TPU v7x, 32 devices: a whole 2x2x4 slice. The times are simulated.
32 devices in a mesh: tm: 4 (over x, core), space: 8 (over z, y).
Axes of the slice: x: 2, y: 2, z: 4, core: 2. Of those that a mesh axis runs over, the one named last changes fastest.
Arguments:
- starts: float32 [4, 32, 256, 384], P('tm', 'space'), may hold values from -18 to 18, as said below
- material: int32 [32, 256, 384], P('space'), may hold values from 0 to 7
- conductivity: float32 [8], replicated, may hold values from 0.3 to 3, as said below
Outputs:
- new_starts: float32 [4, 32, 256, 384], P('tm', 'space')
- coarse_path: float32 [4, 8, 64, 96], P('tm')
Inputs may be any that keep to these rules, and one draw needn't show every extreme that they name: `starts`: start states of order one. `conductivity`: positive conductivities.
All inputs are finite; a program needn't handle non-finite values.
Results may differ from a plain program's by a relative error of at most 0.0001.
Values sent between devices are 32-bit elements; how exact they have to be, the bound alone decides.
A program may use at most 128 MiB of HBM per device.

v0:
```python
import jax
import jax.numpy as jnp
from jax import lax
from jax.sharding import PartitionSpec as P

FACTOR = 4
SUBSTEPS = 2
SWEEPS = 2
JACOBI = 3
fine_step = 0.15
coarse_rate = 0.3
face_offsets = ((0, 1, 1), (2, 1, 1), (1, 0, 1), (1, 2, 1), (1, 1, 0), (1, 1, 2))


def extended(x, sides, width):
    for axis, dim in sides:
        peers, length = (lax.axis_size(axis), x.shape[dim])
        up = [(i, (i + 1) % peers) for i in range(peers - 1)]
        down = [(j, i) for i, j in up]
        last = lax.slice_in_dim(x, length - width, length, axis=dim)
        leading = lax.slice_in_dim(x, 0, width, axis=dim)
        before = lax.ppermute(last, axis, up)
        after = lax.ppermute(leading, axis, down)
        x = jnp.concatenate([before, x, after], axis=dim)
    return x


def shifted(x, axis, by):
    peers = lax.axis_size(axis)
    pairs = [(i, i + by) for i in range(peers) if 0 <= i + by < peers]
    return lax.ppermute(x, axis, pairs)


def window(padded, offsets, cells):
    return padded[
        offsets[0] : offsets[0] + cells[0],
        offsets[1] : offsets[1] + cells[1],
        offsets[2] : offsets[2] + cells[2],
    ]


def laplace_apply(padded, cells):
    summed = jnp.zeros(cells, jnp.float32)
    for shift_x in range(3):
        for shift_y in range(3):
            for shift_z in range(3):
                moved_axes = int(shift_x != 1) + int(shift_y != 1) + int(shift_z != 1)
                if moved_axes == 0:
                    continue
                weight = 0.5 ** (moved_axes - 1)
                summed = summed + weight * window(padded, (shift_x, shift_y, shift_z), cells)
    return 14.0 * window(padded, (1, 1, 1), cells) - summed


def operate(vector, root_cond):
    scaled = root_cond * vector
    padded = extended(scaled, (("space", 0),), 1)
    padded = jnp.pad(padded, ((0, 0), (1, 1), (1, 1)))
    return vector + fine_step * root_cond * laplace_apply(padded, vector.shape)


def grid_squares(resid):
    return lax.psum(jnp.sum(resid * resid), "space")


def grid_curvature(direction, image):
    return lax.psum(jnp.sum(direction * image), "space")


def substep(rhs_field, root_cond):
    iterate = rhs_field
    resid = rhs_field - operate(iterate, root_cond)
    direction = resid
    norm_now = grid_squares(resid)
    for sweep_index in range(SWEEPS):
        image = operate(direction, root_cond)
        step_len = norm_now / grid_curvature(direction, image)
        iterate = iterate + step_len * direction
        resid = resid - step_len * image
        if sweep_index + 1 < SWEEPS:
            norm_next = grid_squares(resid)
            direction = resid + norm_next / norm_now * direction
            norm_now = norm_next
    return iterate


def propagate(start_field, root_cond):
    current = start_field
    for step_index in range(SUBSTEPS):
        current = substep(current, root_cond)
    return current


def restrict(fine_field):
    size_x, size_y, size_z = fine_field.shape
    blocks = fine_field.reshape(
        size_x // FACTOR, FACTOR, size_y // FACTOR, FACTOR, size_z // FACTOR, FACTOR
    )
    return jnp.mean(blocks, axis=(1, 3, 5))


def prolong(coarse_field):
    size_x, size_y, size_z = coarse_field.shape
    spread = jnp.broadcast_to(
        coarse_field[:, None, :, None, :, None], (size_x, FACTOR, size_y, FACTOR, size_z, FACTOR)
    )
    return spread.reshape(size_x * FACTOR, size_y * FACTOR, size_z * FACTOR)


def coarse_setup(coarse_k):
    padded_k = jnp.pad(coarse_k, 1, mode="edge")
    face_coefs = []
    diagonal = jnp.ones(coarse_k.shape, jnp.float32)
    for offsets in face_offsets:
        coef = coarse_rate * 0.5 * (coarse_k + window(padded_k, offsets, coarse_k.shape))
        face_coefs.append(coef)
        diagonal = diagonal + coef
    return (face_coefs, diagonal)


def coarse_step(source, face_coefs, diagonal):
    iterate = source
    for sweep_index in range(JACOBI):
        padded = jnp.pad(iterate, 1)
        summed = jnp.zeros(source.shape, jnp.float32)
        for coef, offsets in zip(face_coefs, face_offsets):
            summed = summed + coef * window(padded, offsets, source.shape)
        iterate = (source + summed) / diagonal
    return iterate


def local(starts, material, conductivity):
    start_field = starts[0]
    conduct = jnp.zeros(start_field.shape, jnp.float32)
    for region in range(conductivity.shape[0]):
        conduct = conduct + jnp.where(material == region, conductivity[region], 0.0)
    root_cond = jnp.sqrt(conduct)
    coarse_start, coarse_k = (
        lax.all_gather(restrict(start_field), "space", axis=0, tiled=True),
        lax.all_gather(restrict(conduct), "space", axis=0, tiled=True),
    )
    face_coefs, diagonal = coarse_setup(coarse_k)
    coarse_old = coarse_step(coarse_start, face_coefs, diagonal)
    fine_end = propagate(start_field, root_cond)
    tm_index = lax.axis_index("tm")
    slice_count = lax.axis_size("tm")
    local_end = restrict(fine_end)
    coarse_end = lax.all_gather(local_end, "space", axis=0, tiled=True)
    jump_term = coarse_end - coarse_old
    coarse_rows = local_end.shape[0]
    carry_start = jnp.where(tm_index == 0, coarse_start, jnp.zeros_like(coarse_start))

    def relay_turn(turn_index, carry_in):
        stepped = coarse_step(carry_in, face_coefs, diagonal) + jump_term
        arrived = shifted(stepped, "tm", 1)
        return jnp.where(tm_index == turn_index + 1, arrived, carry_in)

    carry_own = lax.fori_loop(0, slice_count - 1, relay_turn, carry_start)
    path_own = coarse_step(carry_own, face_coefs, diagonal) + jump_term
    slab_offset = lax.axis_index("space") * coarse_rows
    path_slab = lax.dynamic_slice_in_dim(path_own, slab_offset, coarse_rows, 0)
    corrected = fine_end + prolong(path_slab - local_end)
    received = shifted(corrected, "tm", 1)
    new_field = jnp.where(tm_index == 0, start_field, received)
    return (new_field[None], path_own[None])


def solution(mesh):
    return jax.shard_map(
        local,
        mesh=mesh,
        in_specs=(P("tm", "space", None, None), P("space", None, None), P()),
        out_specs=(P("tm", "space", None, None), P("tm", None, None, None)),
        check_vma=False,
    )
```

profile of v0, /device:TPU:1, one launch (start us, length us, event | category | flops | bytes accessed | tf_op | source)
XLA Modules:
  0.0 589.1 jit_solution(5427695950292236274)
XLA Ops:
  23.5 9.3 %collective-permute-done.1 = f32[1,256,384]{2,1,0:T(8,128)S(1)} collective-permute-done((f32[1,256,384]{2,1,0:T(8,128)S(1)}, f32[1,256,384]{2,1,0:T(8,128)S(1)}, u32[]{:S(2)}, u32[]{:S(2)}) %collective-permute-start.1) | collective-permute-done | bytes 393248 | tf_op jit(solution)/shard_map/ppermute | solution.py:22
  34.6 14.8 %sqrt_multiply_fusion.4 = (f32[4,256,384]{2,1,0:T(8,128)}, f32[4,256,384]{2,1,0:T(8,128)}) fusion(f32[]{:T(128)} %bitcast.8, s32[4,256,384]{2,1,0:T(8,128)} %param.6, f32[]{:T(128)} %bitcast.7, f32[]{:T(128)} %bitcast.6, f32[]{:T(128)} %bitcast.5, f32[]{:T(128)} %bitcast.4, f32[]{:T(128)} %bitcast.3, f32[]{:T(128)} %bitcast.2, f32[]{:T(128)} %bitcast.1, ...), kind=kLoop, calls=%fused_computation.402 | loop fusion | flops 30277632 | bytes 46399520 | tf_op jit(solution)/shard_map/mul | solution.py:56
  74.1 15.3 %multiply_reduce_fusion.4 = (f32[]{:T(128)}, f32[]{:T(128)}, f32[4,256,384]{2,1,0:T(8,128)}) fusion(f32[4,256,384]{2,1,0:T(8,128)} %get-tuple-element.313, f32[6,258,386]{2,1,0:T(8,128)S(1)} %select_maximum_fusion.8, f32[1,256,384]{2,1,0:T(8,128)} %copy-done.29, f32[4,256,384]{2,1,0:T(8,128)} %get-tuple-element.312, f32[1,256,384]{2,1,0:T(8,128)} %copy-done.32, ...), kind=kLoop, calls=%fused_computation.394 | loop fusion | flops 31064064 | bytes 44826664 | tf_op jit(solution)/shard_map/reduce_sum | solution.py:67
  89.3 17.0 %all-reduce.16 = (f32[]{:T(128)}, f32[]{:T(128)}) all-reduce(f32[]{:T(128)} %get-tuple-element.270, f32[]{:T(128)} %get-tuple-element.269), channel_id=1, replica_groups=mesh['tm'=4,'space'=8] {'space'}, use_global_device_ids=true, to_apply=%region_1.2 | all-reduce | flops 2 | bytes 16 | tf_op jit(solution)/shard_map/psum | solution.py:63
  110.6 14.4 %psum.58 = f32[]{:T(128)} all-reduce(f32[]{:T(128)} %multiply_reduce_fusion.3), channel_id=1, replica_groups=mesh['tm'=4,'space'=8] {'space'}, use_global_device_ids=true, to_apply=%region_5.6 | all-reduce | flops 1 | bytes 8 | tf_op jit(solution)/shard_map/psum | solution.py:63
  154.0 14.7 %fusion.43 = f32[]{:T(128)} fusion(f32[6,258,386]{2,1,0:T(8,128)S(1)} %select_maximum_fusion.6, f32[1,256,384]{2,1,0:T(8,128)} %copy-done.33, f32[4,256,384]{2,1,0:T(8,128)} %copy-done.23, f32[1,256,384]{2,1,0:T(8,128)} %copy-done.36, f32[4,256,384]{2,1,0:T(8,128)} %get-tuple-element.313, f32[]{:T(128)S(6)} %div.82, f32[4,256,384]{2,1,0:T(8,128)} %get-tuple-element.311, ...), kind=kLoop, calls=%fused_computation.82 | loop fusion | flops 31850496 | bytes 44826668 | tf_op jit(solution)/shard_map/reduce_sum | solution.py:67
  168.8 16.6 %psum.59 = f32[]{:T(128)} all-reduce(f32[]{:T(128)} %fusion.43), channel_id=1, replica_groups=mesh['tm'=4,'space'=8] {'space'}, use_global_device_ids=true, to_apply=%region_7.8 | all-reduce | flops 1 | bytes 8 | tf_op jit(solution)/shard_map/psum | solution.py:67
  186.7 10.9 %sqrt_multiply_fusion.2 = (f32[4,256,384]{2,1,0:T(8,128)S(1)}, f32[4,256,384]{2,1,0:T(8,128)}) fusion(f32[]{:T(128)} %bitcast.8, s32[4,256,384]{2,1,0:T(8,128)} %param.6, f32[]{:T(128)} %bitcast.7, f32[]{:T(128)} %bitcast.6, f32[]{:T(128)} %bitcast.5, f32[]{:T(128)} %bitcast.4, f32[]{:T(128)} %bitcast.3, f32[]{:T(128)} %bitcast.2, f32[]{:T(128)} %bitcast.1, ...), kind=kLoop, calls=%fused_computation.400 | loop fusion | flops 12582912 | bytes 9437228 | tf_op jit(solution)/shard_map/mul | solution.py:56
  209.5 14.9 %sqrt_multiply_fusion.1 = (f32[4,256,384]{2,1,0:T(8,128)}, f32[4,256,384]{2,1,0:T(8,128)}) fusion(f32[]{:T(128)} %bitcast.8, s32[4,256,384]{2,1,0:T(8,128)} %param.6, f32[]{:T(128)} %bitcast.7, f32[]{:T(128)} %bitcast.6, f32[]{:T(128)} %bitcast.5, f32[]{:T(128)} %bitcast.4, f32[]{:T(128)} %bitcast.3, f32[]{:T(128)} %bitcast.2, f32[]{:T(128)} %bitcast.1, ...), kind=kLoop, calls=%fused_computation.399 | loop fusion | flops 30277632 | bytes 46399520 | tf_op jit(solution)/shard_map/mul | solution.py:56
  232.3 14.7 %reduce_sum.129 = f32[64,4,96,4]{3,2,1,0:T(8,128)} reshape(f32[256,384]{1,0:T(8,128)S(1)} %reduce_sum.128) | data formatting | bytes 786432 | tf_op jit(solution)/shard_map/reduce_sum | solution.py:99
  252.7 24.9 %all-gather = f32[512,96]{1,0:T(8,128)S(1)} all-gather(f32[64,96]{1,0:T(8,128)S(1)} %broadcast_multiply_fusion.2), channel_id=2, replica_groups=mesh['tm'=4,'space'=8] {'space'}, dimensions={0}, use_global_device_ids=true | all-gather | bytes 221184 | tf_op jit(solution)/shard_map/all_gather | solution.py:139
  281.0 15.3 %multiply_reduce_fusion.1 = (f32[]{:T(128)}, f32[]{:T(128)}, f32[4,256,384]{2,1,0:T(8,128)}) fusion(f32[4,256,384]{2,1,0:T(8,128)} %get-tuple-element.308, f32[6,258,386]{2,1,0:T(8,128)S(1)} %select_maximum_fusion.2, f32[1,256,384]{2,1,0:T(8,128)} %copy-done.28, f32[4,256,384]{2,1,0:T(8,128)} %get-tuple-element.307, ...), kind=kLoop, calls=%fused_computation.389 | loop fusion | flops 31064064 | bytes 44826664 | tf_op jit(solution)/shard_map/reduce_sum | solution.py:67
  296.3 17.0 %all-reduce.15 = (f32[]{:T(128)}, f32[]{:T(128)}) all-reduce(f32[]{:T(128)} %get-tuple-element.268, f32[]{:T(128)} %get-tuple-element.267), channel_id=1, replica_groups=mesh['tm'=4,'space'=8] {'space'}, use_global_device_ids=true, to_apply=%region_9.10 | all-reduce | flops 2 | bytes 16 | tf_op jit(solution)/shard_map/psum | solution.py:63
  317.7 14.7 %psum.62 = f32[]{:T(128)} all-reduce(f32[]{:T(128)} %multiply_reduce_fusion), channel_id=1, replica_groups=mesh['tm'=4,'space'=8] {'space'}, use_global_device_ids=true, to_apply=%region_13.14 | all-reduce | flops 1 | bytes 8 | tf_op jit(solution)/shard_map/psum | solution.py:63
  349.9 14.6 %reduce_sum.132 = f32[64,4,96,4]{3,2,1,0:T(8,128)} reshape(f32[256,384]{1,0:T(8,128)S(1)} %copy-done.37) | data formatting | bytes 786432 | tf_op jit(solution)/shard_map/reduce_sum | solution.py:99
  370.3 24.5 %all-gather.1 = f32[512,96]{1,0:T(8,128)S(1)} all-gather(f32[64,96]{1,0:T(8,128)S(1)} %broadcast_multiply_fusion.1), channel_id=3, replica_groups=mesh['tm'=4,'space'=8] {'space'}, dimensions={0}, use_global_device_ids=true | all-gather | bytes 221184 | tf_op jit(solution)/shard_map/all_gather | solution.py:140
  400.2 14.7 %fusion.44 = f32[]{:T(128)} fusion(f32[6,258,386]{2,1,0:T(8,128)S(1)} %select_maximum_fusion, f32[1,256,384]{2,1,0:T(8,128)} %copy-done.27, f32[4,256,384]{2,1,0:T(8,128)} %copy-done.20, f32[1,256,384]{2,1,0:T(8,128)} %collective-permute-done.11, f32[4,256,384]{2,1,0:T(8,128)} %get-tuple-element.308, f32[]{:T(128)S(6)} %div.85, ...), kind=kLoop, calls=%fused_computation.83 | loop fusion | flops 31850496 | bytes 44826668 | tf_op jit(solution)/shard_map/reduce_sum | solution.py:67
  417.4 16.9 %psum.63 = f32[]{:T(128)} all-reduce(f32[]{:T(128)} %fusion.44), channel_id=1, replica_groups=mesh['tm'=4,'space'=8] {'space'}, use_global_device_ids=true, to_apply=%region_15.16 | all-reduce | flops 1 | bytes 8 | tf_op jit(solution)/shard_map/psum | solution.py:67
  439.1 14.6 %reduce_sum.135 = f32[64,4,96,4]{3,2,1,0:T(8,128)} reshape(f32[256,384]{1,0:T(8,128)S(1)} %get-tuple-element.304) | data formatting | bytes 786432 | tf_op jit(solution)/shard_map/reduce_sum | solution.py:99
  459.6 24.5 %all-gather.2 = f32[512,96]{1,0:T(8,128)S(1)} all-gather(f32[64,96]{1,0:T(8,128)S(1)} %broadcast_multiply_fusion), channel_id=4, replica_groups=mesh['tm'=4,'space'=8] {'space'}, dimensions={0}, use_global_device_ids=true | all-gather | bytes 221184 | tf_op jit(solution)/shard_map/all_gather | solution.py:148
  484.5 62.8 %while.15 = (s32[]{:T(128)}, f32[8,64,96]{2,1,0:T(8,128)S(1)}, s32[]{:T(128)}, f32[8,64,96]{2,1,0:T(8,128)S(1)}, f32[8,64,96]{2,1,0:T(8,128)S(1)}, /*index=5*/f3...) while((s32[]{:T(128)}, f32[8,64,96]{2,1,0:T(8,128)S(1)}, ...), condition=%wide.region_23.24_spmd, body=%wide.region_22.23_spmd.sunk | while | flops 2015235 | bytes 7274663 | solution.py:158
  485.3 41.5 %collective-permute-start = (f32[8,64,96]{2,1,0:T(8,128)S(1)}, f32[8,64,96]{2,1,0:T(8,128)S(1)}, u32[]{:S(2)}, u32[]{:S(2)}) collective-permute-start(f32[8,64,96]{2,1,0:T(8,128)S(1)} %fusion.304), channel_id=1, source_target_pairs={{0,8},{8,16},{16,24},{1,9},{9,17},{17,25},{2,10},{10,18},{18,26},{... | collective-permute-start | bytes 589832 | tf_op jit(solution)/shard_map/while/body/eval_jaxpr/ppermute | solution.py:31
  553.8 11.8 %broadcast_in_dim.73 = f32[256,384]{1,0:T(8,128)S(1)} reshape(f32[64,4,96,4]{3,2,1,0:T(8,128)} %broadcast_in_dim.72) | data formatting | bytes 786432 | tf_op jit(solution)/shard_map/broadcast_in_dim | solution.py:104
  570.2 17.3 %collective-permute-done.13 = f32[4,256,384]{2,1,0:T(8,128)S(1)} collective-permute-done((f32[4,256,384]{2,1,0:T(8,128)S(1)}, f32[4,256,384]{2,1,0:T(8,128)S(1)}, u32[]{:S(2)}, u32[]{:S(2)}) %collective-permute-start.13) | collective-permute-done | bytes 1572896 | tf_op jit(solution)/shard_map/ppermute | solution.py:31
  (160 shorter events, 184.7 us)
Async XLA Ops:
  10.7 12.8 %collective-permute-start.2 = (f32[1,256,384]{2,1,0:T(8,128)S(1)}, f32[1,256,384]{2,1,0:T(8,128)S(1)}, u32[]{:S(2)}, u32[]{:S(2)}) collective-permute-start(f32[1,256,384]{2,1,0:T(8,128)S(1)} %get-tuple-element.327), channel_id=1, source_target_pairs={{1,0},{2,1},{3,2},{4,3},{5,4},{6,5},{7,6},{9,8},{10,9},{11,10},{12... | collective-permute-start | bytes 1179656 | tf_op jit(solution)/shard_map/ppermute | solution.py:23
  12.0 20.8 %collective-permute-start.1 = (f32[1,256,384]{2,1,0:T(8,128)S(1)}, f32[1,256,384]{2,1,0:T(8,128)S(1)}, u32[]{:S(2)}, u32[]{:S(2)}) collective-permute-start(f32[1,256,384]{2,1,0:T(8,128)S(1)} %get-tuple-element.326), channel_id=1, source_target_pairs={{0,1},{1,2},{2,3},{3,4},{4,5},{5,6},{6,7},{8,9},{9,10},{10,11},{11... | collective-permute-start | bytes 1179656 | tf_op jit(solution)/shard_map/ppermute | solution.py:22
  50.8 13.2 %collective-permute-start.4 = (f32[1,256,384]{2,1,0:T(8,128)S(1)}, f32[1,256,384]{2,1,0:T(8,128)S(1)}, u32[]{:S(2)}, u32[]{:S(2)}) collective-permute-start(f32[1,256,384]{2,1,0:T(8,128)S(1)} %get-tuple-element.325), channel_id=1, source_target_pairs={{1,0},{2,1},{3,2},{4,3},{5,4},{6,5},{7,6},{9,8},{10,9},{11,10},{12... | collective-permute-start | bytes 1179656 | tf_op jit(solution)/shard_map/ppermute | solution.py:23
  52.1 21.0 %collective-permute-start.3 = (f32[1,256,384]{2,1,0:T(8,128)S(1)}, f32[1,256,384]{2,1,0:T(8,128)S(1)}, u32[]{:S(2)}, u32[]{:S(2)}) collective-permute-start(f32[1,256,384]{2,1,0:T(8,128)S(1)} %get-tuple-element.324), channel_id=1, source_target_pairs={{0,1},{1,2},{2,3},{3,4},{4,5},{5,6},{6,7},{8,9},{9,10},{10,11},{11... | collective-permute-start | bytes 1179656 | tf_op jit(solution)/shard_map/ppermute | solution.py:22
  134.6 8.7 %collective-permute-start.6 = (f32[1,256,384]{2,1,0:T(8,128)S(1)}, f32[1,256,384]{2,1,0:T(8,128)S(1)}, u32[]{:S(2)}, u32[]{:S(2)}) collective-permute-start(f32[1,256,384]{2,1,0:T(8,128)S(1)} %get-tuple-element.323), channel_id=1, source_target_pairs={{1,0},{2,1},{3,2},{4,3},{5,4},{6,5},{7,6},{9,8},{10,9},{11,10},{12... | collective-permute-start | bytes 1179656 | tf_op jit(solution)/shard_map/ppermute | solution.py:23
  135.9 16.4 %collective-permute-start.5 = (f32[1,256,384]{2,1,0:T(8,128)S(1)}, f32[1,256,384]{2,1,0:T(8,128)S(1)}, u32[]{:S(2)}, u32[]{:S(2)}) collective-permute-start(f32[1,256,384]{2,1,0:T(8,128)S(1)} %get-tuple-element.322), channel_id=1, source_target_pairs={{0,1},{1,2},{2,3},{3,4},{4,5},{5,6},{6,7},{8,9},{9,10},{10,11},{11... | collective-permute-start | bytes 1179656 | tf_op jit(solution)/shard_map/ppermute | solution.py:22
  197.6 8.5 %collective-permute-start.8 = (f32[1,256,384]{2,1,0:T(8,128)S(1)}, f32[1,256,384]{2,1,0:T(8,128)S(1)}, u32[]{:S(2)}, u32[]{:S(2)}) collective-permute-start(f32[1,256,384]{2,1,0:T(8,128)S(1)} %get-tuple-element.321), channel_id=1, source_target_pairs={{1,0},{2,1},{3,2},{4,3},{5,4},{6,5},{7,6},{9,8},{10,9},{11,10},{12... | collective-permute-start | bytes 1179656 | tf_op jit(solution)/shard_map/ppermute | solution.py:23
  198.9 9.5 %collective-permute-start.7 = (f32[1,256,384]{2,1,0:T(8,128)S(1)}, f32[1,256,384]{2,1,0:T(8,128)S(1)}, u32[]{:S(2)}, u32[]{:S(2)}) collective-permute-start(f32[1,256,384]{2,1,0:T(8,128)S(1)} %get-tuple-element.320), channel_id=1, source_target_pairs={{0,1},{1,2},{2,3},{3,4},{4,5},{5,6},{6,7},{8,9},{9,10},{10,11},{11... | collective-permute-start | bytes 1179656 | tf_op jit(solution)/shard_map/ppermute | solution.py:22
  225.7 51.9 %collective-permute-start.10 = (f32[1,256,384]{2,1,0:T(8,128)S(1)}, f32[1,256,384]{2,1,0:T(8,128)S(1)}, u32[]{:S(2)}, u32[]{:S(2)}) collective-permute-start(f32[1,256,384]{2,1,0:T(8,128)S(1)} %get-tuple-element.319), channel_id=1, source_target_pairs={{1,0},{2,1},{3,2},{4,3},{5,4},{6,5},{7,6},{9,8},{10,9},{11,10},{12... | collective-permute-start | bytes 1179656 | tf_op jit(solution)/shard_map/ppermute | solution.py:23
  227.0 51.4 %collective-permute-start.9 = (f32[1,256,384]{2,1,0:T(8,128)S(1)}, f32[1,256,384]{2,1,0:T(8,128)}, u32[]{:S(2)}, u32[]{:S(2)}) collective-permute-start(f32[1,256,384]{2,1,0:T(8,128)S(1)} %get-tuple-element.318), channel_id=1, source_target_pairs={{0,1},{1,2},{2,3},{3,4},{4,5},{5,6},{6,7},{8,9},{9,10},{10,11},{11... | collective-permute-start | bytes 1179656 | tf_op jit(solution)/shard_map/ppermute | solution.py:22
  277.6 118.5 %copy-start.25 = (f32[512,96]{1,0:T(8,128)}, f32[512,96]{1,0:T(8,128)S(1)}, u32[]{:S(2)}) copy-start(f32[512,96]{1,0:T(8,128)S(1)} %all-gather) | copy-start | bytes 589828
  343.8 53.3 %collective-permute-start.12 = (f32[1,256,384]{2,1,0:T(8,128)S(1)}, f32[1,256,384]{2,1,0:T(8,128)S(1)}, u32[]{:S(2)}, u32[]{:S(2)}) collective-permute-start(f32[1,256,384]{2,1,0:T(8,128)S(1)} %get-tuple-element.317), channel_id=1, source_target_pairs={{1,0},{2,1},{3,2},{4,3},{5,4},{6,5},{7,6},{9,8},{10,9},{11,10},{12... | collective-permute-start | bytes 1179656 | tf_op jit(solution)/shard_map/ppermute | solution.py:23
  345.1 52.8 %collective-permute-start.11 = (f32[1,256,384]{2,1,0:T(8,128)S(1)}, f32[1,256,384]{2,1,0:T(8,128)}, u32[]{:S(2)}, u32[]{:S(2)}) collective-permute-start(f32[1,256,384]{2,1,0:T(8,128)S(1)} %get-tuple-element.316), channel_id=1, source_target_pairs={{0,1},{1,2},{2,3},{3,4},{4,5},{5,6},{6,7},{8,9},{9,10},{10,11},{11... | collective-permute-start | bytes 1179656 | tf_op jit(solution)/shard_map/ppermute | solution.py:22
  453.7 30.4 %copy-start.3 = (f32[8,64,96]{2,1,0:T(8,128)S(1)}, f32[8,64,96]{2,1,0:T(8,128)}, u32[]{:S(2)}) copy-start(f32[8,64,96]{2,1,0:T(8,128)} %copy-done.2) | copy-start | bytes 589828
  453.7 30.4 %copy-start.5 = (f32[8,64,96]{2,1,0:T(8,128)S(1)}, f32[8,64,96]{2,1,0:T(8,128)}, u32[]{:S(2)}) copy-start(f32[8,64,96]{2,1,0:T(8,128)} %copy-done.4) | copy-start | bytes 589828
  453.7 30.4 %copy-start.7 = (f32[8,64,96]{2,1,0:T(8,128)S(1)}, f32[8,64,96]{2,1,0:T(8,128)}, u32[]{:S(2)}) copy-start(f32[8,64,96]{2,1,0:T(8,128)} %copy-done.6) | copy-start | bytes 589828
  453.7 30.4 %copy-start.9 = (f32[8,64,96]{2,1,0:T(8,128)S(1)}, f32[8,64,96]{2,1,0:T(8,128)}, u32[]{:S(2)}) copy-start(f32[8,64,96]{2,1,0:T(8,128)} %copy-done.8) | copy-start | bytes 589828
  453.7 30.4 %copy-start.11 = (f32[8,64,96]{2,1,0:T(8,128)S(1)}, f32[8,64,96]{2,1,0:T(8,128)}, u32[]{:S(2)}) copy-start(f32[8,64,96]{2,1,0:T(8,128)} %copy-done.10) | copy-start | bytes 589828
  453.7 30.4 %copy-start.26 = (f32[512,96]{1,0:T(8,128)S(1)}, f32[512,96]{1,0:T(8,128)}, u32[]{:S(2)}) copy-start(f32[512,96]{1,0:T(8,128)} %copy-done.25) | copy-start | bytes 589828
  459.6 24.9 %copy-start.12 = (f32[8,64,96]{2,1,0:T(8,128)S(1)}, f32[8,64,96]{2,1,0:T(8,128)}, u32[]{:S(2)}) copy-start(f32[8,64,96]{2,1,0:T(8,128)} %get-tuple-element.420) | copy-start | bytes 589828
  485.3 44.8 %collective-permute-start = (f32[8,64,96]{2,1,0:T(8,128)S(1)}, f32[8,64,96]{2,1,0:T(8,128)S(1)}, u32[]{:S(2)}, u32[]{:S(2)}) collective-permute-start(f32[8,64,96]{2,1,0:T(8,128)S(1)} %fusion.304), channel_id=1, source_target_pairs={{0,8},{8,16},{16,24},{1,9},{9,17},{17,25},{2,10},{10,18},{18,26},{... | collective-permute-start | bytes 589832 | tf_op jit(solution)/shard_map/while/body/eval_jaxpr/ppermute | solution.py:31
  530.9 7.7 %collective-permute-start = (f32[8,64,96]{2,1,0:T(8,128)S(1)}, f32[8,64,96]{2,1,0:T(8,128)S(1)}, u32[]{:S(2)}, u32[]{:S(2)}) collective-permute-start(f32[8,64,96]{2,1,0:T(8,128)S(1)} %fusion.304), channel_id=1, source_target_pairs={{0,8},{8,16},{16,24},{1,9},{9,17},{17,25},{2,10},{10,18},{18,26},{... | collective-permute-start | bytes 589832 | tf_op jit(solution)/shard_map/while/body/eval_jaxpr/ppermute | solution.py:31
  539.5 7.7 %collective-permute-start = (f32[8,64,96]{2,1,0:T(8,128)S(1)}, f32[8,64,96]{2,1,0:T(8,128)S(1)}, u32[]{:S(2)}, u32[]{:S(2)}) collective-permute-start(f32[8,64,96]{2,1,0:T(8,128)S(1)} %fusion.304), channel_id=1, source_target_pairs={{0,8},{8,16},{16,24},{1,9},{9,17},{17,25},{2,10},{10,18},{18,26},{... | collective-permute-start | bytes 589832 | tf_op jit(solution)/shard_map/while/body/eval_jaxpr/ppermute | solution.py:31
  565.7 21.9 %collective-permute-start.13 = (f32[4,256,384]{2,1,0:T(8,128)S(1)}, f32[4,256,384]{2,1,0:T(8,128)S(1)}, u32[]{:S(2)}, u32[]{:S(2)}) collective-permute-start(f32[4,256,384]{2,1,0:T(8,128)S(1)} %broadcast_add_fusion), channel_id=1, source_target_pairs={{0,8},{8,16},{16,24},{1,9},{9,17},{17,25},{2,10},{10,18},{18,26},{... | collective-permute-start | bytes 4718600 | tf_op jit(solution)/shard_map/ppermute | solution.py:31
  (31 other events, 271.3 us)
where the time goes:
time: 598 us; the launch traced here: 589 us
  other arithmetic  172 us (29%)
  blocking collectives  171 us (29%)
  starting transfers between devices  90.2 us (15%)
  waiting for transfers between devices  77.1 us (13%)
  local copies, waits for them, and re-layouts  70.3 us (12%)
  between operations  9.11 us (2%)
    psum x4, blocking collectives, grid_squares(): return lax.psum(jnp.sum(resid * resid), 'space')  63.1 us
    reduce_sum x4, other arithmetic, grid_curvature(): return lax.psum(jnp.sum(direction * image), 'space')  60.1 us
    mul x5, other arithmetic, operate(): scaled = root_cond * vector  57.2 us
    ppermute x4, starting transfers between devices, shifted(): return lax.ppermute(x, axis, pairs)  54.8 us
    reduce_sum x3, local copies, waits for them, and re-layouts, restrict(): return jnp.mean(blocks, axis=(1, 3, 5))  43.9 us
    psum x2, blocking collectives, grid_curvature(): return lax.psum(jnp.sum(direction * image), 'space')  33.5 us
    reduce_sum x6, other arithmetic, restrict(): return jnp.mean(blocks, axis=(1, 3, 5))  29.9 us
    ppermute x6, waiting for transfers between devices, extended(): before = lax.ppermute(last, axis, up)  29.7 us
  transfers between devices with their start and end apart: 16, of which 12 were waited for; matrix products, arithmetic and copies ran while one was open for 7% of the time, Pallas kernels for 0%

commit v1 on v0

--- a/solution.py
+++ b/solution.py
@@ -145,7 +145,15 @@
     tm_index = lax.axis_index("tm")
     slice_count = lax.axis_size("tm")
     local_end = restrict(fine_end)
-    coarse_end = lax.all_gather(local_end, "space", axis=0, tiled=True)
+    ways, here, hop = (lax.axis_size("space"), lax.axis_index("space"), local_end.shape[0])
+    line, have = (local_end, 1)
+    while have < ways:
+        line = jnp.concatenate(
+            [line, lax.ppermute(line, "space", [(d, (d - have) % ways) for d in range(ways)])],
+            axis=0,
+        )
+        have = 2 * have
+    coarse_end = jnp.roll(line, here * hop, axis=0)
     jump_term = coarse_end - coarse_old
     coarse_rows = local_end.shape[0]
     carry_start = jnp.where(tm_index == 0, coarse_start, jnp.zeros_like(coarse_start))

time: 598 us -> 583 us (0.975)
  blocking collectives: 171 us -> 150 us
    all_gather x1 -> x0, blocking collectives: 24.5 us -> none  [local(): coarse_end = lax.all_gather(local_end, 'space', axis=0, tiled=True)]
    ppermute x6, waiting for transfers between devices: 20.2 us -> 0.02 us  [extended(): after = lax.ppermute(leading, axis, down)]
    ppermute x6, waiting for transfers between devices: 29.7 us -> 43.8 us  [extended(): before = lax.ppermute(last, axis, up)]
    ppermute x0 -> x3, waiting for transfers between devices: none -> 11.2 us  [local(): lax.ppermute(line, 'space', [(d, (d - have) % ways) for d in range(ways)])]
  transfers between devices with their start and end apart: 16 -> 19, of which waited for: 12 -> 11; matrix products, arithmetic and copies ran while one was open for 7% -> 8% of each run, Pallas kernels for 0% -> 0%
where the time goes in v1:
time: 583 us; the launch traced here: 574 us
  other arithmetic  172 us (30%)
  blocking collectives  150 us (26%)
  starting transfers between devices  87.1 us (15%)
  waiting for transfers between devices  82.2 us (14%)
  local copies, waits for them, and re-layouts  72.4 us (12%)
  between operations  9.25 us (2%)
    psum x4, blocking collectives, grid_squares(): return lax.psum(jnp.sum(resid * resid), 'space')  66.6 us
    reduce_sum x4, other arithmetic, grid_curvature(): return lax.psum(jnp.sum(direction * image), 'space')  60.5 us
    mul x5, other arithmetic, operate(): scaled = root_cond * vector  57.5 us
    ppermute x4, starting transfers between devices, shifted(): return lax.ppermute(x, axis, pairs)  55.1 us
    reduce_sum x3, local copies, waits for them, and re-layouts, restrict(): return jnp.mean(blocks, axis=(1, 3, 5))  44 us
    ppermute x6, waiting for transfers between devices, extended(): before = lax.ppermute(last, axis, up)  43.8 us
    psum x2, blocking collectives, grid_curvature(): return lax.psum(jnp.sum(direction * image), 'space')  32.6 us
    reduce_sum x6, other arithmetic, restrict(): return jnp.mean(blocks, axis=(1, 3, 5))  29.9 us
  transfers between devices with their start and end apart: 19, of which 11 were waited for; matrix products, arithmetic and copies ran while one was open for 8% of the time, Pallas kernels for 0%

profile of v1, /device:TPU:1, one launch (start us, length us, event | category | flops | bytes accessed | tf_op | source)
XLA Modules:
  0.0 573.8 jit_solution(4308228425982850501)
XLA Ops:
  16.1 14.9 %collective-permute-done.1 = f32[1,256,384]{2,1,0:T(8,128)S(1)} collective-permute-done((f32[1,256,384]{2,1,0:T(8,128)S(1)}, f32[1,256,384]{2,1,0:T(8,128)S(1)}, u32[]{:S(2)}, u32[]{:S(2)}) %collective-permute-start.1) | collective-permute-done | bytes 393248 | tf_op jit(solution)/shard_map/ppermute | solution.py:22
  33.5 15.0 %sqrt_multiply_fusion.4 = (f32[4,256,384]{2,1,0:T(8,128)}, f32[4,256,384]{2,1,0:T(8,128)}) fusion(f32[]{:T(128)} %bitcast.8, s32[4,256,384]{2,1,0:T(8,128)} %param.6, f32[]{:T(128)} %bitcast.7, f32[]{:T(128)} %bitcast.6, f32[]{:T(128)} %bitcast.5, f32[]{:T(128)} %bitcast.4, f32[]{:T(128)} %bitcast.3, f32[]{:T(128)} %bitcast.2, f32[]{:T(128)} %bitcast.1, ...), kind=kLoop, calls=%fused_computation.402 | loop fusion | flops 30277632 | bytes 46399520 | tf_op jit(solution)/shard_map/mul | solution.py:56
  55.2 13.9 %collective-permute-done.3 = f32[1,256,384]{2,1,0:T(8,128)S(1)} collective-permute-done((f32[1,256,384]{2,1,0:T(8,128)S(1)}, f32[1,256,384]{2,1,0:T(8,128)S(1)}, u32[]{:S(2)}, u32[]{:S(2)}) %collective-permute-start.3) | collective-permute-done | bytes 393248 | tf_op jit(solution)/shard_map/ppermute | solution.py:22
  70.2 15.4 %multiply_reduce_fusion.4 = (f32[]{:T(128)}, f32[]{:T(128)}, f32[4,256,384]{2,1,0:T(8,128)}) fusion(f32[4,256,384]{2,1,0:T(8,128)} %get-tuple-element.313, f32[6,258,386]{2,1,0:T(8,128)S(1)} %select_maximum_fusion.8, f32[1,256,384]{2,1,0:T(8,128)} %copy-done.32, f32[4,256,384]{2,1,0:T(8,128)} %get-tuple-element.312, f32[1,256,384]{2,1,0:T(8,128)} %copy-done.29, ...), kind=kLoop, calls=%fused_computation.394 | loop fusion | flops 31064064 | bytes 44826664 | tf_op jit(solution)/shard_map/reduce_sum | solution.py:67
  85.6 21.7 %all-reduce.16 = (f32[]{:T(128)}, f32[]{:T(128)}) all-reduce(f32[]{:T(128)} %get-tuple-element.270, f32[]{:T(128)} %get-tuple-element.269), channel_id=1, replica_groups=mesh['tm'=4,'space'=8] {'space'}, use_global_device_ids=true, to_apply=%region_1.2 | all-reduce | flops 2 | bytes 16 | tf_op jit(solution)/shard_map/psum | solution.py:63
  111.7 14.4 %psum.58 = f32[]{:T(128)} all-reduce(f32[]{:T(128)} %multiply_reduce_fusion.3), channel_id=1, replica_groups=mesh['tm'=4,'space'=8] {'space'}, use_global_device_ids=true, to_apply=%region_5.6 | all-reduce | flops 1 | bytes 8 | tf_op jit(solution)/shard_map/psum | solution.py:63
  150.7 14.9 %fusion.43 = f32[]{:T(128)} fusion(f32[6,258,386]{2,1,0:T(8,128)S(1)} %select_maximum_fusion.6, f32[1,256,384]{2,1,0:T(8,128)} %copy-done.36, f32[4,256,384]{2,1,0:T(8,128)} %copy-done.23, f32[1,256,384]{2,1,0:T(8,128)} %copy-done.33, f32[4,256,384]{2,1,0:T(8,128)} %get-tuple-element.313, f32[]{:T(128)S(6)} %div.82, f32[4,256,384]{2,1,0:T(8,128)} %get-tuple-element.311, ...), kind=kLoop, calls=%fused_computation.82 | loop fusion | flops 31850496 | bytes 44826668 | tf_op jit(solution)/shard_map/reduce_sum | solution.py:67
  165.6 17.0 %psum.59 = f32[]{:T(128)} all-reduce(f32[]{:T(128)} %fusion.43), channel_id=1, replica_groups=mesh['tm'=4,'space'=8] {'space'}, use_global_device_ids=true, to_apply=%region_7.8 | all-reduce | flops 1 | bytes 8 | tf_op jit(solution)/shard_map/psum | solution.py:67
  183.8 11.0 %sqrt_multiply_fusion.2 = (f32[4,256,384]{2,1,0:T(8,128)S(1)}, f32[4,256,384]{2,1,0:T(8,128)}) fusion(f32[]{:T(128)} %bitcast.8, s32[4,256,384]{2,1,0:T(8,128)} %param.6, f32[]{:T(128)} %bitcast.7, f32[]{:T(128)} %bitcast.6, f32[]{:T(128)} %bitcast.5, f32[]{:T(128)} %bitcast.4, f32[]{:T(128)} %bitcast.3, f32[]{:T(128)} %bitcast.2, f32[]{:T(128)} %bitcast.1, ...), kind=kLoop, calls=%fused_computation.400 | loop fusion | flops 12582912 | bytes 9437228 | tf_op jit(solution)/shard_map/mul | solution.py:56
  208.4 14.9 %sqrt_multiply_fusion.1 = (f32[4,256,384]{2,1,0:T(8,128)}, f32[4,256,384]{2,1,0:T(8,128)}) fusion(f32[]{:T(128)} %bitcast.8, s32[4,256,384]{2,1,0:T(8,128)} %param.6, f32[]{:T(128)} %bitcast.7, f32[]{:T(128)} %bitcast.6, f32[]{:T(128)} %bitcast.5, f32[]{:T(128)} %bitcast.4, f32[]{:T(128)} %bitcast.3, f32[]{:T(128)} %bitcast.2, f32[]{:T(128)} %bitcast.1, ...), kind=kLoop, calls=%fused_computation.399 | loop fusion | flops 30277632 | bytes 46399520 | tf_op jit(solution)/shard_map/mul | solution.py:56
  231.2 14.7 %reduce_sum.129 = f32[64,4,96,4]{3,2,1,0:T(8,128)} reshape(f32[256,384]{1,0:T(8,128)S(1)} %reduce_sum.128) | data formatting | bytes 786432 | tf_op jit(solution)/shard_map/reduce_sum | solution.py:99
  251.6 24.9 %all-gather = f32[512,96]{1,0:T(8,128)S(1)} all-gather(f32[64,96]{1,0:T(8,128)S(1)} %broadcast_multiply_fusion.1), channel_id=2, replica_groups=mesh['tm'=4,'space'=8] {'space'}, dimensions={0}, use_global_device_ids=true | all-gather | bytes 221184 | tf_op jit(solution)/shard_map/all_gather | solution.py:139
  279.9 15.4 %multiply_reduce_fusion.1 = (f32[]{:T(128)}, f32[]{:T(128)}, f32[4,256,384]{2,1,0:T(8,128)}) fusion(f32[4,256,384]{2,1,0:T(8,128)} %get-tuple-element.308, f32[6,258,386]{2,1,0:T(8,128)S(1)} %select_maximum_fusion.2, f32[1,256,384]{2,1,0:T(8,128)} %copy-done.27, f32[4,256,384]{2,1,0:T(8,128)} %get-tuple-element.307, ...), kind=kLoop, calls=%fused_computation.389 | loop fusion | flops 31064064 | bytes 44826664 | tf_op jit(solution)/shard_map/reduce_sum | solution.py:67
  295.3 15.5 %all-reduce.15 = (f32[]{:T(128)}, f32[]{:T(128)}) all-reduce(f32[]{:T(128)} %get-tuple-element.268, f32[]{:T(128)} %get-tuple-element.267), channel_id=1, replica_groups=mesh['tm'=4,'space'=8] {'space'}, use_global_device_ids=true, to_apply=%region_9.10 | all-reduce | flops 2 | bytes 16 | tf_op jit(solution)/shard_map/psum | solution.py:63
  315.2 15.0 %psum.62 = f32[]{:T(128)} all-reduce(f32[]{:T(128)} %multiply_reduce_fusion), channel_id=1, replica_groups=mesh['tm'=4,'space'=8] {'space'}, use_global_device_ids=true, to_apply=%region_13.14 | all-reduce | flops 1 | bytes 8 | tf_op jit(solution)/shard_map/psum | solution.py:63
  346.1 14.7 %reduce_sum.132 = f32[64,4,96,4]{3,2,1,0:T(8,128)} reshape(f32[256,384]{1,0:T(8,128)S(1)} %copy-done.37) | data formatting | bytes 786432 | tf_op jit(solution)/shard_map/reduce_sum | solution.py:99
  366.6 26.1 %all-gather.1 = f32[512,96]{1,0:T(8,128)S(1)} all-gather(f32[64,96]{1,0:T(8,128)S(1)} %broadcast_multiply_fusion), channel_id=3, replica_groups=mesh['tm'=4,'space'=8] {'space'}, dimensions={0}, use_global_device_ids=true | all-gather | bytes 221184 | tf_op jit(solution)/shard_map/all_gather | solution.py:140
  398.1 14.8 %fusion.44 = f32[]{:T(128)} fusion(f32[6,258,386]{2,1,0:T(8,128)S(1)} %select_maximum_fusion, f32[1,256,384]{2,1,0:T(8,128)} %collective-permute-done.12, f32[4,256,384]{2,1,0:T(8,128)} %copy-done.20, f32[1,256,384]{2,1,0:T(8,128)} %copy-done.28, f32[4,256,384]{2,1,0:T(8,128)} %get-tuple-element.308, f32[]{:T(128)S(6)} %div.85, ...), kind=kLoop, calls=%fused_computation.83 | loop fusion | flops 31850496 | bytes 44826668 | tf_op jit(solution)/shard_map/reduce_sum | solution.py:67
  415.3 15.7 %psum.63 = f32[]{:T(128)} all-reduce(f32[]{:T(128)} %fusion.44), channel_id=1, replica_groups=mesh['tm'=4,'space'=8] {'space'}, use_global_device_ids=true, to_apply=%region_15.16 | all-reduce | flops 1 | bytes 8 | tf_op jit(solution)/shard_map/psum | solution.py:67
  435.8 14.6 %reduce_sum.135 = f32[64,4,96,4]{3,2,1,0:T(8,128)} reshape(f32[256,384]{1,0:T(8,128)S(1)} %get-tuple-element.304) | data formatting | bytes 786432 | tf_op jit(solution)/shard_map/reduce_sum | solution.py:99
  468.9 63.1 %while.15 = (s32[]{:T(128)}, f32[8,64,96]{2,1,0:T(8,128)S(1)}, s32[]{:T(128)}, f32[8,64,96]{2,1,0:T(8,128)S(1)}, f32[8,64,96]{2,1,0:T(8,128)S(1)}, /*index=5*/f3...) while((s32[]{:T(128)}, f32[8,64,96]{2,1,0:T(8,128)S(1)}, ...), condition=%wide.region_23.24_spmd, body=%wide.region_22.23_spmd.sunk | while | flops 2015235 | bytes 7274663 | solution.py:166
  469.7 41.8 %collective-permute-start = (f32[8,64,96]{2,1,0:T(8,128)S(1)}, f32[8,64,96]{2,1,0:T(8,128)S(1)}, u32[]{:S(2)}, u32[]{:S(2)}) collective-permute-start(f32[8,64,96]{2,1,0:T(8,128)S(1)} %fusion.303), channel_id=1, source_target_pairs={{0,8},{8,16},{16,24},{1,9},{9,17},{17,25},{2,10},{10,18},{18,26},{... | collective-permute-start | bytes 589832 | tf_op jit(solution)/shard_map/while/body/eval_jaxpr/ppermute | solution.py:31
  538.5 11.8 %broadcast_in_dim.73 = f32[256,384]{1,0:T(8,128)S(1)} reshape(f32[64,4,96,4]{3,2,1,0:T(8,128)} %broadcast_in_dim.72) | data formatting | bytes 786432 | tf_op jit(solution)/shard_map/broadcast_in_dim | solution.py:104
  554.9 17.3 %collective-permute-done.16 = f32[4,256,384]{2,1,0:T(8,128)S(1)} collective-permute-done((f32[4,256,384]{2,1,0:T(8,128)S(1)}, f32[4,256,384]{2,1,0:T(8,128)S(1)}, u32[]{:S(2)}, u32[]{:S(2)}) %collective-permute-start.16) | collective-permute-done | bytes 1572896 | tf_op jit(solution)/shard_map/ppermute | solution.py:31
  (175 shorter events, 169.1 us)
Async XLA Ops:
  10.7 20.3 %copy-start.22 = (f32[4,256,384]{2,1,0:T(8,128)}, f32[4,256,384]{2,1,0:T(8,128)S(1)}, u32[]{:S(2)}) copy-start(f32[4,256,384]{2,1,0:T(8,128)S(1)} %bitcast_multiply_fusion) | copy-start | bytes 4718596
  10.8 20.2 %collective-permute-start.1 = (f32[1,256,384]{2,1,0:T(8,128)S(1)}, f32[1,256,384]{2,1,0:T(8,128)S(1)}, u32[]{:S(2)}, u32[]{:S(2)}) collective-permute-start(f32[1,256,384]{2,1,0:T(8,128)S(1)} %get-tuple-element.326), channel_id=1, source_target_pairs={{0,1},{1,2},{2,3},{3,4},{4,5},{5,6},{6,7},{8,9},{9,10},{10,11},{11... | collective-permute-start | bytes 1179656 | tf_op jit(solution)/shard_map/ppermute | solution.py:22
  14.8 16.2 %collective-permute-start.2 = (f32[1,256,384]{2,1,0:T(8,128)S(1)}, f32[1,256,384]{2,1,0:T(8,128)S(1)}, u32[]{:S(2)}, u32[]{:S(2)}) collective-permute-start(f32[1,256,384]{2,1,0:T(8,128)S(1)} %get-tuple-element.327), channel_id=1, source_target_pairs={{1,0},{2,1},{3,2},{4,3},{5,4},{6,5},{7,6},{9,8},{10,9},{11,10},{12... | collective-permute-start | bytes 1179656 | tf_op jit(solution)/shard_map/ppermute | solution.py:23
  48.5 20.7 %copy-start.18 = (f32[4,256,384]{2,1,0:T(8,128)S(1)}, f32[4,256,384]{2,1,0:T(8,128)}, u32[]{:S(2)}) copy-start(f32[4,256,384]{2,1,0:T(8,128)} %get-tuple-element.312) | copy-start | bytes 4718596
  49.7 19.4 %collective-permute-start.3 = (f32[1,256,384]{2,1,0:T(8,128)S(1)}, f32[1,256,384]{2,1,0:T(8,128)S(1)}, u32[]{:S(2)}, u32[]{:S(2)}) collective-permute-start(f32[1,256,384]{2,1,0:T(8,128)S(1)} %get-tuple-element.324), channel_id=1, source_target_pairs={{0,1},{1,2},{2,3},{3,4},{4,5},{5,6},{6,7},{8,9},{9,10},{10,11},{11... | collective-permute-start | bytes 1179656 | tf_op jit(solution)/shard_map/ppermute | solution.py:22
  53.9 15.3 %collective-permute-start.4 = (f32[1,256,384]{2,1,0:T(8,128)S(1)}, f32[1,256,384]{2,1,0:T(8,128)S(1)}, u32[]{:S(2)}, u32[]{:S(2)}) collective-permute-start(f32[1,256,384]{2,1,0:T(8,128)S(1)} %get-tuple-element.325), channel_id=1, source_target_pairs={{1,0},{2,1},{3,2},{4,3},{5,4},{6,5},{7,6},{9,8},{10,9},{11,10},{12... | collective-permute-start | bytes 1179656 | tf_op jit(solution)/shard_map/ppermute | solution.py:23
  135.7 12.4 %collective-permute-start.5 = (f32[1,256,384]{2,1,0:T(8,128)S(1)}, f32[1,256,384]{2,1,0:T(8,128)S(1)}, u32[]{:S(2)}, u32[]{:S(2)}) collective-permute-start(f32[1,256,384]{2,1,0:T(8,128)S(1)} %get-tuple-element.322), channel_id=1, source_target_pairs={{0,1},{1,2},{2,3},{3,4},{4,5},{5,6},{6,7},{8,9},{9,10},{10,11},{11... | collective-permute-start | bytes 1179656 | tf_op jit(solution)/shard_map/ppermute | solution.py:22
  139.2 8.9 %collective-permute-start.6 = (f32[1,256,384]{2,1,0:T(8,128)S(1)}, f32[1,256,384]{2,1,0:T(8,128)S(1)}, u32[]{:S(2)}, u32[]{:S(2)}) collective-permute-start(f32[1,256,384]{2,1,0:T(8,128)S(1)} %get-tuple-element.323), channel_id=1, source_target_pairs={{1,0},{2,1},{3,2},{4,3},{5,4},{6,5},{7,6},{9,8},{10,9},{11,10},{12... | collective-permute-start | bytes 1179656 | tf_op jit(solution)/shard_map/ppermute | solution.py:23
  194.8 12.6 %collective-permute-start.7 = (f32[1,256,384]{2,1,0:T(8,128)S(1)}, f32[1,256,384]{2,1,0:T(8,128)S(1)}, u32[]{:S(2)}, u32[]{:S(2)}) collective-permute-start(f32[1,256,384]{2,1,0:T(8,128)S(1)} %get-tuple-element.320), channel_id=1, source_target_pairs={{0,1},{1,2},{2,3},{3,4},{4,5},{5,6},{6,7},{8,9},{9,10},{10,11},{11... | collective-permute-start | bytes 1179656 | tf_op jit(solution)/shard_map/ppermute | solution.py:22
  198.5 8.9 %collective-permute-start.8 = (f32[1,256,384]{2,1,0:T(8,128)S(1)}, f32[1,256,384]{2,1,0:T(8,128)S(1)}, u32[]{:S(2)}, u32[]{:S(2)}) collective-permute-start(f32[1,256,384]{2,1,0:T(8,128)S(1)} %get-tuple-element.321), channel_id=1, source_target_pairs={{1,0},{2,1},{3,2},{4,3},{5,4},{6,5},{7,6},{9,8},{10,9},{11,10},{12... | collective-permute-start | bytes 1179656 | tf_op jit(solution)/shard_map/ppermute | solution.py:23
  224.6 51.9 %collective-permute-start.10 = (f32[1,256,384]{2,1,0:T(8,128)S(1)}, f32[1,256,384]{2,1,0:T(8,128)S(1)}, u32[]{:S(2)}, u32[]{:S(2)}) collective-permute-start(f32[1,256,384]{2,1,0:T(8,128)S(1)} %get-tuple-element.319), channel_id=1, source_target_pairs={{1,0},{2,1},{3,2},{4,3},{5,4},{6,5},{7,6},{9,8},{10,9},{11,10},{12... | collective-permute-start | bytes 1179656 | tf_op jit(solution)/shard_map/ppermute | solution.py:23
  225.9 51.4 %collective-permute-start.9 = (f32[1,256,384]{2,1,0:T(8,128)S(1)}, f32[1,256,384]{2,1,0:T(8,128)}, u32[]{:S(2)}, u32[]{:S(2)}) collective-permute-start(f32[1,256,384]{2,1,0:T(8,128)S(1)} %get-tuple-element.318), channel_id=1, source_target_pairs={{0,1},{1,2},{2,3},{3,4},{4,5},{5,6},{6,7},{8,9},{9,10},{10,11},{11... | collective-permute-start | bytes 1179656 | tf_op jit(solution)/shard_map/ppermute | solution.py:22
  276.5 117.5 %copy-start.25 = (f32[512,96]{1,0:T(8,128)}, f32[512,96]{1,0:T(8,128)S(1)}, u32[]{:S(2)}) copy-start(f32[512,96]{1,0:T(8,128)S(1)} %all-gather) | copy-start | bytes 589828
  341.7 53.4 %collective-permute-start.11 = (f32[1,256,384]{2,1,0:T(8,128)S(1)}, f32[1,256,384]{2,1,0:T(8,128)S(1)}, u32[]{:S(2)}, u32[]{:S(2)}) collective-permute-start(f32[1,256,384]{2,1,0:T(8,128)S(1)} %get-tuple-element.316), channel_id=1, source_target_pairs={{0,1},{1,2},{2,3},{3,4},{4,5},{5,6},{6,7},{8,9},{9,10},{10,11},{11... | collective-permute-start | bytes 1179656 | tf_op jit(solution)/shard_map/ppermute | solution.py:22
  344.8 51.0 %collective-permute-start.12 = (f32[1,256,384]{2,1,0:T(8,128)S(1)}, f32[1,256,384]{2,1,0:T(8,128)}, u32[]{:S(2)}, u32[]{:S(2)}) collective-permute-start(f32[1,256,384]{2,1,0:T(8,128)S(1)} %get-tuple-element.317), channel_id=1, source_target_pairs={{1,0},{2,1},{3,2},{4,3},{5,4},{6,5},{7,6},{9,8},{10,9},{11,10},{12... | collective-permute-start | bytes 1179656 | tf_op jit(solution)/shard_map/ppermute | solution.py:23
  412.9 19.3 %copy-start.15 = (f32[4,256,384]{2,1,0:T(8,128)S(1)}, f32[4,256,384]{2,1,0:T(8,128)}, u32[]{:S(2)}) copy-start(f32[4,256,384]{2,1,0:T(8,128)} %get-tuple-element.308) | copy-start | bytes 4718596
  456.2 2.8 collective-permute-start.13
  459.1 3.2 collective-permute-start.14
  462.3 5.6 collective-permute-start.15
  469.7 45.1 %collective-permute-start = (f32[8,64,96]{2,1,0:T(8,128)S(1)}, f32[8,64,96]{2,1,0:T(8,128)S(1)}, u32[]{:S(2)}, u32[]{:S(2)}) collective-permute-start(f32[8,64,96]{2,1,0:T(8,128)S(1)} %fusion.303), channel_id=1, source_target_pairs={{0,8},{8,16},{16,24},{1,9},{9,17},{17,25},{2,10},{10,18},{18,26},{... | collective-permute-start | bytes 589832 | tf_op jit(solution)/shard_map/while/body/eval_jaxpr/ppermute | solution.py:31
  515.7 7.7 %collective-permute-start = (f32[8,64,96]{2,1,0:T(8,128)S(1)}, f32[8,64,96]{2,1,0:T(8,128)S(1)}, u32[]{:S(2)}, u32[]{:S(2)}) collective-permute-start(f32[8,64,96]{2,1,0:T(8,128)S(1)} %fusion.303), channel_id=1, source_target_pairs={{0,8},{8,16},{16,24},{1,9},{9,17},{17,25},{2,10},{10,18},{18,26},{... | collective-permute-start | bytes 589832 | tf_op jit(solution)/shard_map/while/body/eval_jaxpr/ppermute | solution.py:31
  524.3 7.7 %collective-permute-start = (f32[8,64,96]{2,1,0:T(8,128)S(1)}, f32[8,64,96]{2,1,0:T(8,128)S(1)}, u32[]{:S(2)}, u32[]{:S(2)}) collective-permute-start(f32[8,64,96]{2,1,0:T(8,128)S(1)} %fusion.303), channel_id=1, source_target_pairs={{0,8},{8,16},{16,24},{1,9},{9,17},{17,25},{2,10},{10,18},{18,26},{... | collective-permute-start | bytes 589832 | tf_op jit(solution)/shard_map/while/body/eval_jaxpr/ppermute | solution.py:31
  550.3 22.0 %copy-start.17 = (f32[1,4,256,384]{3,2,1,0:T(8,128)S(1)}, f32[1,4,256,384]{3,2,1,0:T(8,128)}, u32[]{:S(2)}) copy-start(f32[1,4,256,384]{3,2,1,0:T(8,128)} %param.5) | copy-start | bytes 4718596
  550.4 21.9 %collective-permute-start.16 = (f32[4,256,384]{2,1,0:T(8,128)S(1)}, f32[4,256,384]{2,1,0:T(8,128)S(1)}, u32[]{:S(2)}, u32[]{:S(2)}) collective-permute-start(f32[4,256,384]{2,1,0:T(8,128)S(1)} %broadcast_add_fusion), channel_id=1, source_target_pairs={{0,8},{8,16},{16,24},{1,9},{9,17},{17,25},{2,10},{10,18},{18,26},{... | collective-permute-start | bytes 4718600 | tf_op jit(solution)/shard_map/ppermute | solution.py:31
  (34 other events, 227.8 us)
